TPU v7x, 32 devices: a whole 2x2x4 slice. The times are simulated.
32 devices in a mesh: dp: 8 (over y, x, core), tp: 4 (over z).
Axes of the slice: x: 2, y: 2, z: 4, core: 2. Of those that a mesh axis runs over, the one named last changes fastest.
Arguments:
- residual_hidden: bfloat16 [64, 4096], P('dp'), may hold values from -6 to 6
- attention_norm_gain: float32 [4096], replicated, may hold values from 0.25 to 1.75
- query_matrix: bfloat16 [4096, 8192], P(None, 'tp'), may hold values from -0.09375 to 0.09375
- key_matrix: bfloat16 [4096, 1024], P(None, 'tp'), may hold values from -0.09375 to 0.09375
- value_matrix: bfloat16 [4096, 1024], P(None, 'tp'), may hold values from -0.09375 to 0.09375
- output_matrix: bfloat16 [8192, 4096], P('tp'), may hold values from -0.5 to 0.5
- query_adapter_down: bfloat16 [4096, 64], P(('dp', 'tp')), may hold values from -0.09375 to 0.09375
- query_adapter_up: bfloat16 [64, 8192], P(None, ('tp', 'dp')), may hold values from -0.375 to 0.375
- output_adapter_down: bfloat16 [8192, 64], P(('tp', 'dp')), may hold values from -0.5 to 0.5
- output_adapter_up: bfloat16 [64, 4096], P(None, ('tp', 'dp')), may hold values from -0.375 to 0.375
- cached_rotated_keys: bfloat16 [64, 8, 1024, 128], P('dp', 'tp'), as said below
- cached_value_rows: bfloat16 [64, 8, 1024, 128], P('dp', 'tp'), may hold values from -6 to 6
- cache_fill_lengths: int32 [64], P('dp'), may hold values from 1 to 1024, 32768 in all
Outputs:
- attn_out: float32 [64, 4096], P('dp', 'tp')
Inputs may be any that keep to these rules, and one draw needn't show every extreme that they name: Cache positions at or above a row's length hold no key of that row; the new token stands at position cache_fill_lengths. `cached_rotated_keys`: keys are already rotated to their positions.
All inputs are finite; a program needn't handle non-finite values. No bound on the sum of `cache_fill_lengths` on one device may be relied on, other than what follows from the above.
Results may differ from a plain program's by a relative error of at most 0.004.
The roundings to bfloat16 on the way count: a program that leaves them out, or rounds other values in their place, can miss the bound.
Values may be sent and summed in bfloat16 or wider, within the bound.
A program may use at most 128 MiB of HBM per device.

v0:
```python
import math

import jax
import jax.numpy as jnp
from jax import lax
from jax.sharding import PartitionSpec as P

HEAD_SIZE = 128


adapter_scale = 2.0
rope_theta = 500000.0


def rotate(vectors, positions):
    half_dim = vectors.shape[-1] // 2
    steps_idx = jnp.arange(half_dim, dtype=jnp.float32)
    inverse = jnp.exp(steps_idx * (-2.0 * math.log(rope_theta) / vectors.shape[-1]))
    angles = positions[:, None, None] * inverse[None, None, :]
    cosine = jnp.cos(angles)
    sine = jnp.sin(angles)
    first = vectors[..., :half_dim]
    second = vectors[..., half_dim:]
    return jnp.concatenate(
        [first * cosine - second * sine, second * cosine + first * sine], axis=-1
    )


def on_device(
    residual_hidden,
    attention_norm_gain,
    query_matrix,
    key_matrix,
    value_matrix,
    output_matrix,
    query_adapter_down,
    query_adapter_up,
    output_adapter_down,
    output_adapter_up,
    cached_rotated_keys,
    cached_value_rows,
    cache_fill_lengths,
):
    row_count = residual_hidden.shape[0]
    feature_width = residual_hidden.shape[1]
    rank_width = query_adapter_down.shape[1]
    local_heads = query_matrix.shape[1] // HEAD_SIZE
    local_groups = key_matrix.shape[1] // HEAD_SIZE
    group_size = local_heads // local_groups
    cache_length = cached_rotated_keys.shape[2]
    hidden_f = residual_hidden.astype(jnp.float32)
    normalized_hidden = (
        hidden_f
        * lax.rsqrt(jnp.mean(hidden_f * hidden_f, axis=-1, keepdims=True) + 1e-05)
        * attention_norm_gain
    ).astype(jnp.bfloat16)
    q_up_local, o_down_local = (
        lax.all_gather(query_adapter_up, "dp", axis=1, tiled=True),
        lax.all_gather(output_adapter_down, "dp", axis=0, tiled=True),
    )
    q_down_share = lax.all_gather(query_adapter_down, "dp", axis=0, tiled=True)
    dp_count = lax.axis_size("dp")
    tp_count = lax.axis_size("tp")
    block_width = feature_width // (dp_count * tp_count)
    picked = lax.dynamic_index_in_dim(
        normalized_hidden.reshape(row_count, dp_count, tp_count, block_width),
        lax.axis_index("tp"),
        2,
        keepdims=False,
    )
    partial_low = jnp.einsum(
        "rdb,dbk->rk",
        picked,
        q_down_share.reshape(dp_count, block_width, rank_width),
        preferred_element_type=jnp.float32,
    )
    query_low_rank = lax.psum(partial_low, "tp")
    query_rows = jnp.dot(
        normalized_hidden, query_matrix, preferred_element_type=jnp.float32
    ) + adapter_scale * jnp.dot(
        query_low_rank, q_up_local.astype(jnp.float32), precision=lax.Precision.HIGHEST
    )
    keys_new = jnp.dot(normalized_hidden, key_matrix, preferred_element_type=jnp.float32)
    values_new = jnp.dot(
        normalized_hidden, value_matrix, preferred_element_type=jnp.float32
    ).astype(jnp.bfloat16)
    positions = cache_fill_lengths.astype(jnp.float32)
    query_rot = (
        rotate(query_rows.reshape(row_count, local_heads, HEAD_SIZE), positions)
        .astype(jnp.bfloat16)
        .reshape(row_count, local_groups, group_size, HEAD_SIZE)
    )
    key_rot = rotate(keys_new.reshape(row_count, local_groups, HEAD_SIZE), positions).astype(
        jnp.bfloat16
    )
    value_rows = values_new.reshape(row_count, local_groups, HEAD_SIZE)
    score_scale = HEAD_SIZE ** (-0.5)
    scores = (
        jnp.einsum(
            "rkgd,rkcd->rkgc", query_rot, cached_rotated_keys, preferred_element_type=jnp.float32
        )
        * score_scale
    )
    visible = (
        jnp.arange(cache_length, dtype=jnp.int32)[None, None, None, :]
        < cache_fill_lengths[:, None, None, None]
    )
    scores = jnp.where(visible, scores, -jnp.inf)
    own_score = (
        jnp.einsum("rkgd,rkd->rkg", query_rot, key_rot, preferred_element_type=jnp.float32)
        * score_scale
    )
    top_score = jnp.maximum(jnp.max(scores, axis=-1), own_score)
    cache_exp = jnp.exp(scores - top_score[..., None])
    own_exp = jnp.exp(own_score - top_score)
    denominator = jnp.sum(cache_exp, axis=-1) + own_exp
    cache_weight = (cache_exp / denominator[..., None]).astype(jnp.bfloat16)
    own_weight = (own_exp / denominator).astype(jnp.bfloat16)
    attn = jnp.einsum(
        "rkgc,rkcd->rkgd", cache_weight, cached_value_rows, preferred_element_type=jnp.float32
    )
    attn = (
        attn
        + own_weight.astype(jnp.float32)[..., None] * value_rows.astype(jnp.float32)[:, :, None, :]
    )
    attention_flattened = attn.astype(jnp.bfloat16).reshape(row_count, local_heads * HEAD_SIZE)
    low_o_part = jnp.dot(attention_flattened, o_down_local, preferred_element_type=jnp.float32)
    base_contribution = jnp.dot(
        attention_flattened, output_matrix, preferred_element_type=jnp.float32
    )
    output_low_rank = lax.psum(low_o_part, "tp")
    o_up_own = lax.all_gather(output_adapter_up, "dp", axis=1, tiled=True)
    attn_out = lax.psum_scatter(
        base_contribution, "tp", scatter_dimension=1, tiled=True
    ) + adapter_scale * jnp.dot(
        output_low_rank, o_up_own.astype(jnp.float32), precision=lax.Precision.HIGHEST
    )
    return attn_out


def solution(mesh):
    in_specs = (
        P("dp", None),
        P(),
        P(None, "tp"),
        P(None, "tp"),
        P(None, "tp"),
        P("tp", None),
        P(("dp", "tp"), None),
        P(None, ("tp", "dp")),
        P(("tp", "dp"), None),
        P(None, ("tp", "dp")),
        P("dp", "tp", None, None),
        P("dp", "tp", None, None),
        P("dp"),
    )
    out_specs = P("dp", "tp")
    return jax.shard_map(
        on_device, mesh=mesh, in_specs=in_specs, out_specs=out_specs, check_vma=False
    )
```

profile of v0, /device:TPU:0, one launch (start us, length us, event | category | flops | bytes accessed | tf_op | source)
XLA Modules:
  0.0 93.0 jit_solution(13245572097140604651)
XLA Ops:
  6.5 0.0 copy-start
  6.5 0.0 reduce-scatter.2.cloned.1.call-start
  6.5 0.8 convert_element_type.41
  7.4 0.7 iota_compare_fusion
  8.1 1.0 %fusion.11 = f32[8]{0:T(128)S(1)} fusion(bf16[8,4096]{1,0:T(8,128)(2,1)} %param.13), kind=kLoop, calls=%fused_computation.22 | loop fusion | flops 98296 | bytes 65568 | tf_op jit(solution)/shard_map/reduce_sum | solution.py:54
  9.1 10.7 %all_gather.12 = bf16[1024,64]{0,1:T(8,128)(2,1)S(1)} all-gather(bf16[128,64]{0,1:T(8,128)(2,1)} %param.19), channel_id=1, replica_groups=mesh['dp'=8,'tp'=4] {'dp'}, dimensions={0}, use_global_device_ids=true | all-gather | bytes 147456 | tf_op jit(solution)/shard_map/all_gather | solution.py:61
  19.8 0.9 fusion.13
  20.7 0.1 convolution_bitcast_fusion.1
  20.8 11.9 %psum.14 = f32[8,64]{1,0:T(8,128)S(1)} all-reduce(f32[8,64]{1,0:T(8,128)S(1)} %convolution_bitcast_fusion.1), channel_id=1, replica_groups=mesh['dp'=8,'tp'=4] {'tp'}, use_global_device_ids=true, to_apply=%region_1.2 | all-reduce | flops 512 | bytes 4096 | tf_op jit(solution)/shard_map/psum | solution.py:77
  32.8 0.0 copy-start.3
  32.8 0.0 copy-start.1
  32.8 0.0 slice-start
  32.8 0.0 slice-start.1
  32.8 0.0 slice-start.2
  32.8 8.2 %fusion.32 = f32[8,2048]{1,0:T(8,128)S(1)} fusion(bf16[8,4096]{1,0:T(8,128)(2,1)S(1)} %fusion.13, bf16[4096,2048]{1,0:T(8,128)(2,1)} %param.15), kind=kOutput, calls=%fused_computation.59 | convolution fusion | flops 134217728 | bytes 16908288 | tf_op jit(solution)/shard_map/dot_general | solution.py:78
  41.0 0.0 copy-done.3
  41.0 9.9 %all_gather.13 = bf16[64,2048]{1,0:T(8,128)(2,1)S(1)} all-gather(bf16[64,256]{1,0:T(8,128)(2,1)S(1)} %copy-done.3), channel_id=1, replica_groups=mesh['dp'=8,'tp'=4] {'dp'}, dimensions={1}, use_global_device_ids=true | all-gather | bytes 294912 | tf_op jit(solution)/shard_map/all_gather | solution.py:58
  50.9 0.0 copy-done
  50.9 0.0 copy-start.2
  50.9 0.4 convolution_bitcast_fusion
  51.3 0.1 multiply_cosine_fusion
  51.4 0.0 copy-start.6
  51.4 0.2 fusion.2
  51.7 0.1 subtract_convert_fusion
  51.8 0.1 subtract_convert_fusion.1
  51.9 0.1 maximum_bitcast_fusion
  51.9 0.2 fusion.24
  52.1 0.0 copy-done.1
  52.1 0.0 slice-start.3
  52.2 1.3 %fusion.31 = (f32[8,2,8]{2,1,0:T(2,128)S(1)}, f32[8,2,8,1024]{3,2,1,0:T(8,128)S(1)}) fusion(bf16[8,2,1024,128]{3,2,1,0:T(8,128)(2,1)S(1)} %copy-done.1, bf16[8,2,8,64]{3,2,1,0:T(8,128)(2,1)S(1)} %get-tuple-element.15, bf16[8,2,8,64]{3,2,1,0:T(8,128)(2,1)S(1)} %get-tuple-element.16, pred[8,1024]{1,0:T(8,128)(4,1)S(1)} %iota_compare_fusion), kind=kOutput, calls=%fused_computation.58 | convolution fusion | flops 34013056 | bytes 4760064 | tf_op jit(solution)/shard_map/rkgd,rkcd->rkgc/dot_general | solution.py:99
  53.5 0.2 fusion.8
  53.8 0.0 copy-done.2
  53.8 0.4 fusion.7
  54.2 0.0 copy-done.6
  54.2 0.7 fusion.5
  54.9 0.0 slice-done
  54.9 0.0 slice-done.1
  54.9 0.0 slice-done.2
  54.9 0.2 slice-done.3
  55.1 0.0 copy-start.4
  55.2 0.0 copy-start.5
  55.2 2.9 %fusion.18 = f32[8,4096]{1,0:T(8,128)} fusion(bf16[2048,4096]{1,0:T(8,128)(2,1)S(1)} %bitcast.53, bf16[1,8,16,128]{3,2,1,0:T(8,128)(2,1)S(1)} %fusion.5), kind=kOutput, calls=%fused_computation.31 | convolution fusion | flops 134217728 | bytes 16941056 | tf_op jit(solution)/shard_map/dot_general | solution.py:128
  58.1 0.0 reduce-scatter.2.cloned.1.call-update
  58.1 0.0 copy-done.4
  58.1 9.0 %all_gather.14 = bf16[2048,64]{0,1:T(8,128)(2,1)S(1)} all-gather(bf16[256,64]{0,1:T(8,128)(2,1)S(1)} %copy-done.4), channel_id=1, replica_groups=mesh['dp'=8,'tp'=4] {'dp'}, dimensions={0}, use_global_device_ids=true | all-gather | bytes 294912 | tf_op jit(solution)/shard_map/all_gather | solution.py:59
  67.1 0.2 fusion.16
  67.3 8.4 %psum.15 = f32[8,64]{1,0:T(8,128)S(1)} all-reduce(f32[8,64]{1,0:T(8,128)S(1)} %fusion.16), channel_id=1, replica_groups=mesh['dp'=8,'tp'=4] {'tp'}, use_global_device_ids=true, to_apply=%region_5.6 | all-reduce | flops 512 | bytes 4096 | tf_op jit(solution)/shard_map/psum | solution.py:131
  75.7 0.0 copy-done.5
  75.7 8.9 %all_gather.15 = bf16[64,1024]{1,0:T(8,128)(2,1)S(1)} all-gather(bf16[64,128]{1,0:T(8,128)(2,1)S(1)} %copy-done.5), channel_id=1, replica_groups=mesh['dp'=8,'tp'=4] {'dp'}, dimensions={1}, use_global_device_ids=true | all-gather | bytes 147456 | tf_op jit(solution)/shard_map/all_gather | solution.py:132
  84.6 0.0 reduce-scatter.2.cloned.1.call-done
  84.6 1.5 %fusion.4 = f32[8,1024]{1,0:T(8,128)} fusion(f32[8,1024]{1,0:T(8,128)} %reduce-scatter.2.cloned.1.call-done, f32[8,64]{1,0:T(8,128)S(1)} %psum.15, bf16[64,1024]{1,0:T(8,128)(2,1)S(1)} %all_gather.15), kind=kOutput, calls=%fused_computation.8 | convolution fusion | flops 6307840 | bytes 198656 | tf_op jit(solution)/shard_map/dot_general | solution.py:135
  (7 shorter events, 0.1 us)
Async XLA Ops:
  6.5 44.4 %copy-start = (bf16[4096,256]{1,0:T(8,128)(2,1)S(1)}, bf16[4096,256]{1,0:T(8,128)(2,1)}, u32[]{:S(2)}) copy-start(bf16[4096,256]{1,0:T(8,128)(2,1)} %param.16) | copy-start | bytes 6291460
  6.5 78.0 %reduce-scatter.2.cloned.1.call-start = ((), (), s32[]{:S(2)}) async-start(), calls=%async_computation.1 | async-start | bytes 163840 | tf_op jit(solution)/shard_map/reduce_scatter | solution.py:133
  32.8 8.2 %copy-start.3 = (bf16[64,256]{1,0:T(8,128)(2,1)S(1)}, bf16[64,256]{1,0:T(8,128)(2,1)}, u32[]{:S(2)}) copy-start(bf16[64,256]{1,0:T(8,128)(2,1)} %param.20) | copy-start | bytes 98308
  32.8 19.4 %copy-start.1 = (bf16[8,2,1024,128]{3,2,1,0:T(8,128)(2,1)S(1)}, bf16[8,2,1024,128]{3,2,1,0:T(8,128)(2,1)}, u32[]{:S(2)}) copy-start(bf16[8,2,1024,128]{3,2,1,0:T(8,128)(2,1)} %param.23) | copy-start | bytes 12582916
  32.8 22.1 %slice-start = ((s8[16777216]{0:T(1024)(128)(4,1)}), s8[4194304]{0:T(1024)(128)(4,1)S(1)}, s32[]{:S(2)}) async-start(s8[16777216]{0:T(1024)(128)(4,1)} %bitcast.52), calls=%async_computation.2 | async-start | bytes 8388608
  32.8 22.1 %slice-start.1 = ((s8[16777216]{0:T(1024)(128)(4,1)}), s8[4194304]{0:T(1024)(128)(4,1)S(1)}, s32[]{:S(2)}) async-start(s8[16777216]{0:T(1024)(128)(4,1)} %bitcast.52), calls=%async_computation.3 | async-start | bytes 8388608
  32.8 22.1 %slice-start.2 = ((s8[16777216]{0:T(1024)(128)(4,1)}), s8[4194304]{0:T(1024)(128)(4,1)S(1)}, s32[]{:S(2)}) async-start(s8[16777216]{0:T(1024)(128)(4,1)} %bitcast.52), calls=%async_computation.4 | async-start | bytes 8388608
  50.9 2.8 %copy-start.2 = (bf16[4096,256]{1,0:T(8,128)(2,1)S(1)}, bf16[4096,256]{1,0:T(8,128)(2,1)}, u32[]{:S(2)}) copy-start(bf16[4096,256]{1,0:T(8,128)(2,1)} %param.17) | copy-start | bytes 6291460
  51.4 2.7 %copy-start.6 = (bf16[8,2,1024,128]{3,2,1,0:T(8,128)(2,1)S(1)}, bf16[8,2,1024,128]{3,2,1,0:T(8,128)(2,1)}, u32[]{:S(2)}) copy-start(bf16[8,2,1024,128]{3,2,1,0:T(8,128)(2,1)} %param.24) | copy-start | bytes 12582916
  52.1 3.0 %slice-start.3 = ((s8[16777216]{0:T(1024)(128)(4,1)}), s8[4194304]{0:T(1024)(128)(4,1)S(1)}, s32[]{:S(2)}) async-start(s8[16777216]{0:T(1024)(128)(4,1)} %bitcast.52), calls=%async_computation.5 | async-start | bytes 8388608
  55.1 3.0 %copy-start.4 = (bf16[256,64]{0,1:T(8,128)(2,1)S(1)}, bf16[256,64]{0,1:T(8,128)(2,1)}, u32[]{:S(2)}) copy-start(bf16[256,64]{0,1:T(8,128)(2,1)} %param.21) | copy-start | bytes 98308
  55.2 20.5 %copy-start.5 = (bf16[64,128]{1,0:T(8,128)(2,1)S(1)}, bf16[64,128]{1,0:T(8,128)(2,1)}, u32[]{:S(2)}) copy-start(bf16[64,128]{1,0:T(8,128)(2,1)} %param.22) | copy-start | bytes 49156
Sparse Core Ops, SparseCore 0:
  58.2 16.4 reduce-scatter.1
where the time goes:
time: 93.4 us; the launch traced here: 93 us
  blocking collectives  58.8 us (63%)
  matrix products  16.2 us (17%)
  between operations  13.5 us (14%)
  other arithmetic  4.09 us (4%)
    psum x1, blocking collectives, on_device(): query_low_rank = lax.psum(partial_low, 'tp')  11.9 us
    all_gather x1, blocking collectives, on_device(): q_down_share = lax.all_gather(query_adapter_down, 'dp', axis=0, tiled=True)  10.7 us
    all_gather x1, blocking collectives, on_device(): lax.all_gather(query_adapter_up, 'dp', axis=1, tiled=True)  9.91 us
    all_gather x1, blocking collectives, on_device(): lax.all_gather(output_adapter_down, 'dp', axis=0, tiled=True)  9.03 us
    all_gather x1, blocking collectives, on_device(): o_up_own = lax.all_gather(output_adapter_up, 'dp', axis=1, tiled=True)  8.9 us
    psum x1, blocking collectives, on_device(): output_low_rank = lax.psum(low_o_part, 'tp')  8.37 us
    dot_general x1, matrix products, on_device(): jnp.dot(normalized_hidden, query_matrix, preferred_element_type=jnp.float32)  8.19 us
    dot_general x1, matrix products, on_device(): jnp.dot(attention_flattened, output_matrix, preferred_element_type=jnp.fl...  2.92 us
  transfers between devices with their start and end apart: 1, of which 0 were waited for; matrix products, arithmetic and copies ran while one was open for 0% of the time, Pallas kernels for 0%

commit v1 on v0

--- a/solution.py
+++ b/solution.py
@@ -1,8 +1,11 @@
+import functools
 import math
 
 import jax
 import jax.numpy as jnp
 from jax import lax
+from jax.experimental import pallas as pl
+from jax.experimental.pallas import tpu as pltpu
 from jax.sharding import PartitionSpec as P
 
 HEAD_SIZE = 128
@@ -26,7 +29,7 @@
     )
 
 
-def on_device(
+def on_device_narrow(
     residual_hidden,
     attention_norm_gain,
     query_matrix,
@@ -138,6 +141,451 @@
     return attn_out
 
 
+def three_parts(values):
+    high = values.astype(jnp.bfloat16)
+    rest = values - high.astype(jnp.float32)
+    middle = rest.astype(jnp.bfloat16)
+    low = (rest - middle.astype(jnp.float32)).astype(jnp.bfloat16)
+    return jnp.concatenate(
+        [high.astype(jnp.float32), middle.astype(jnp.float32), low.astype(jnp.float32)], axis=0
+    ).astype(jnp.bfloat16)
+
+
+def wide_product(parts, right, rows):
+    product = jnp.dot(parts, right, preferred_element_type=jnp.float32)
+    return product[:rows] + (product[rows : 2 * rows] + product[2 * rows :])
+
+
+def kernel(
+    dp,
+    tp,
+    x_hbm,
+    gain_hbm,
+    table_hbm,
+    wq_hbm,
+    wk_hbm,
+    wv_hbm,
+    wo_hbm,
+    qd_hbm,
+    qu_hbm,
+    od_hbm,
+    ou_hbm,
+    k_hbm,
+    v_hbm,
+    out_ref,
+    x_s,
+    gain_s,
+    table_s,
+    wq_s,
+    wk_s,
+    wv_s,
+    wo_s,
+    qd_s,
+    qu_s,
+    od_s,
+    ou_s,
+    k_s,
+    v_s,
+    normed_s,
+    q_s,
+    key_s,
+    value_s,
+    attn_s,
+    low_send,
+    low_recv,
+    share_send,
+    share_recv,
+    in_sem,
+    w_sem,
+    kv_sem,
+    wo_sem,
+    own_sem,
+    gather_send,
+    gather_recv,
+    low_send_sem,
+    low_recv_sem,
+    share_send_sem,
+    share_recv_sem,
+):
+    d = lax.axis_index("dp")
+    t = lax.axis_index("tp")
+    rows, features = x_hbm.shape
+    rank = qd_hbm.shape[1]
+    groups = k_hbm.shape[1]
+    cache = k_hbm.shape[2]
+    width = wq_hbm.shape[1]
+    heads = width // HEAD_SIZE
+    per_group = heads // groups
+    pieces = w_sem.shape[1]
+    depth = features // pieces
+    columns = out_ref.shape[1]
+    f32, bf16 = jnp.float32, jnp.bfloat16
+
+    small = [
+        pltpu.make_async_copy(src, dst, in_sem.at[i])
+        for i, (src, dst) in enumerate(((x_hbm, x_s), (gain_hbm, gain_s), (table_hbm, table_s)))
+    ]
+    for copy in small:
+        copy.start()
+
+    def weight_copies(k):
+        span = pl.ds(pl.multiple_of(k * depth, depth), depth)
+        return [
+            pltpu.make_async_copy(src.at[span], dst.at[span], w_sem.at[i, k])
+            for i, (src, dst) in enumerate(((wq_hbm, wq_s), (wk_hbm, wk_s), (wv_hbm, wv_s)))
+        ]
+
+    def cache_copies(r):
+        return [
+            pltpu.make_async_copy(src.at[r], dst.at[r], kv_sem.at[i, r])
+            for i, (src, dst) in enumerate(((k_hbm, k_s), (v_hbm, v_s)))
+        ]
+
+    def out_copy(step):
+        to = lax.rem(t + 1 + step, tp)
+        return pltpu.make_async_copy(
+            wo_hbm.at[:, pl.ds(pl.multiple_of(to * columns, columns), columns)],
+            wo_s.at[step],
+            wo_sem.at[step],
+        )
+
+    for k in range(pieces):
+        for copy in weight_copies(k):
+            copy.start()
+
+    factors = ((qd_hbm, qd_s), (qu_hbm, qu_s), (od_hbm, od_s), (ou_hbm, ou_s))
+    own = [
+        pltpu.make_async_copy(src, dst.at[d], own_sem.at[i]) for i, (src, dst) in enumerate(factors)
+    ]
+    for copy in own:
+        copy.start()
+
+    barrier = pltpu.get_barrier_semaphore()
+    for i in range(1, dp):
+        pl.semaphore_signal(
+            barrier,
+            inc=1,
+            device_id=(lax.rem(d + i, dp), t),
+            device_id_type=pl.DeviceIdType.MESH,
+        )
+    for i in range(1, tp):
+        pl.semaphore_signal(
+            barrier,
+            inc=1,
+            device_id=(d, lax.rem(t + i, tp)),
+            device_id_type=pl.DeviceIdType.MESH,
+        )
+
+    for copy in small:
+        copy.wait()
+    hidden = x_s[...].astype(f32)
+    normed_s[...] = (
+        hidden
+        * lax.rsqrt(jnp.mean(hidden * hidden, axis=-1, keepdims=True) + 1e-05)
+        * gain_s[...]
+    ).astype(bf16)
+
+    pl.semaphore_wait(barrier, dp - 1 + tp - 1)
+
+    def gather(which, i):
+        src, dst = factors[which]
+        return pltpu.make_async_remote_copy(
+            src_ref=src,
+            dst_ref=dst.at[d],
+            send_sem=gather_send.at[which, i],
+            recv_sem=gather_recv.at[which, i],
+            device_id=(lax.rem(d + i, dp), t),
+            device_id_type=pl.DeviceIdType.MESH,
+        )
+
+    def arrived(which, i):
+        src, dst = factors[which]
+        return pltpu.make_async_remote_copy(
+            src_ref=src,
+            dst_ref=dst.at[lax.rem(d + dp - i, dp)],
+            send_sem=gather_send.at[which, i],
+            recv_sem=gather_recv.at[which, i],
+            device_id=(lax.rem(d + i, dp), t),
+            device_id_type=pl.DeviceIdType.MESH,
+        )
+
+    for which in range(len(factors)):
+        for i in range(1, dp):
+            gather(which, i).start()
+
+    def take(which):
+        own[which].wait()
+        for i in range(1, dp):
+            arrived(which, i).wait_recv()
+
+    def project(k, totals):
+        for copy in weight_copies(k):
+            copy.wait()
+        for copy in cache_copies(k):
+            copy.start()
+        span = pl.ds(pl.multiple_of(k * depth, depth), depth)
+        block = normed_s[:, span]
+        return tuple(
+            total + jnp.dot(block, weight[span, :], preferred_element_type=f32)
+            for total, weight in zip(totals, (wq_s, wk_s, wv_s))
+        )
+
+    totals = tuple(jnp.zeros((rows, w.shape[1]), f32) for w in (wq_s, wk_s, wv_s))
+    totals = lax.fori_loop(0, pieces // 2, project, totals)
+
+    take(0)
+    part_width = qd_hbm.shape[0]
+    part = jnp.zeros((rows, rank), f32)
+    for i in range(dp):
+        at = pl.multiple_of((i * tp + t) * part_width, part_width)
+        part += jnp.dot(
+            normed_s[:, pl.ds(at, part_width)], qd_s[i], preferred_element_type=f32
+        )
+    low_send[...] = jnp.concatenate(
+        [part, jnp.zeros((rows, HEAD_SIZE - rank), f32)], axis=1
+    )
+
+    def low_copy(step):
+        return pltpu.make_async_remote_copy(
+            src_ref=low_send,
+            dst_ref=low_recv.at[step],
+            send_sem=low_send_sem.at[step],
+            recv_sem=low_recv_sem.at[step],
+            device_id=(d, lax.rem(t + 1 + step, tp)),
+            device_id_type=pl.DeviceIdType.MESH,
+        )
+
+    for step in range(tp - 1):
+        low_copy(step).start()
+
+    totals = lax.fori_loop(pieces // 2, pieces, project, totals)
+    query_total, key_total, value_total = totals
+    for step in range(tp):
+        out_copy(step).start()
+
+    cosine = table_s[:, :HEAD_SIZE]
+    sine = table_s[:, HEAD_SIZE : 2 * HEAD_SIZE]
+
+    def turned(vectors):
+        rolled = pltpu.roll(vectors, HEAD_SIZE // 2, 1)
+        return (vectors * cosine + rolled * sine).astype(bf16).astype(f32)
+
+    for g in range(groups):
+        span = slice(g * HEAD_SIZE, (g + 1) * HEAD_SIZE)
+        key_s[:, g, :] = turned(key_total[:, span])
+        value_s[:, g, :] = value_total[:, span].astype(bf16).astype(f32)
+
+    key_s[:, groups, :] = table_s[:, 2 * HEAD_SIZE :]
+
+    take(1)
+    low = low_send[...]
+    for step in range(tp - 1):
+        low_copy(step).wait_recv()
+        low += low_recv[step]
+    parts = three_parts(low[:, :rank])
+    up_width = qu_hbm.shape[1]
+    for i in range(dp):
+        extra = wide_product(parts, qu_s[i], rows)
+        for j in range(up_width // HEAD_SIZE):
+            h = i * (up_width // HEAD_SIZE) + j
+            base = query_total[:, h * HEAD_SIZE : (h + 1) * HEAD_SIZE]
+            q_s[:, h, :] = turned(
+                base + adapter_scale * extra[:, j * HEAD_SIZE : (j + 1) * HEAD_SIZE]
+            )
+
+    scale = HEAD_SIZE ** (-0.5)
+    at_once = 2
+
+    def attend(step, carry):
+        for u in range(at_once):
+            for copy in cache_copies(step * at_once + u):
+                copy.wait()
+        place = lax.broadcasted_iota(jnp.int32, (per_group, cache), 1).astype(f32)
+        results = []
+        for u in range(at_once):
+            r = step * at_once + u
+            length = key_s[r, groups : groups + 1, :][:, :1]
+            for g in range(groups):
+                query = q_s[r, g * per_group : (g + 1) * per_group, :]
+                scores = (
+                    lax.dot_general(
+                        query.astype(bf16),
+                        k_s[r, g],
+                        (((1,), (1,)), ((), ())),
+                        preferred_element_type=f32,
+                    )
+                    * scale
+                )
+                scores = jnp.where(place < length, scores, -jnp.inf)
+                mine = (
+                    jnp.sum(query * key_s[r, g : g + 1, :], axis=-1, keepdims=True) * scale
+                )
+                top = jnp.maximum(jnp.max(scores, axis=-1, keepdims=True), mine)
+                powers = jnp.exp(scores - top)
+                my_power = jnp.exp(mine - top)
+                inverse = 1.0 / (jnp.sum(powers, axis=-1, keepdims=True) + my_power)
+                weights = (powers * inverse).astype(bf16)
+                my_weight = (my_power * inverse).astype(bf16).astype(f32)
+                mixed = jnp.dot(weights, v_s[r, g], preferred_element_type=f32)
+                mixed = mixed + my_weight * value_s[r, g : g + 1, :]
+                results.append((r, g, mixed.astype(bf16).astype(f32)))
+        for r, g, mixed in results:
+            attn_s[g * per_group : (g + 1) * per_group, r, :] = mixed
+        return carry
+
+    lax.fori_loop(0, rows // at_once, attend, 0)
+
+    flat = jnp.concatenate([attn_s[h] for h in range(heads)], axis=1).astype(bf16)
+
+    take(2)
+    down_rows = od_hbm.shape[0]
+    low_o = jnp.zeros((rows, rank), f32)
+    for i in range(dp):
+        low_o += jnp.dot(
+            flat[:, i * down_rows : (i + 1) * down_rows], od_s[i], preferred_element_type=f32
+        )
+    low_o = jnp.concatenate([low_o, jnp.zeros((rows, HEAD_SIZE - rank), f32)], axis=1)
+
+    def share_copy(step):
+        return pltpu.make_async_remote_copy(
+            src_ref=share_send.at[step],
+            dst_ref=share_recv.at[step],
+            send_sem=share_send_sem.at[step],
+            recv_sem=share_recv_sem.at[step],
+            device_id=(d, lax.rem(t + 1 + step, tp)),
+            device_id_type=pl.DeviceIdType.MESH,
+        )
+
+    tile = 256
+    for step in range(tp):
+        out_copy(step).wait()
+
+        def columns_of(c, carry, step=step):
+            span = pl.ds(pl.multiple_of(c * tile, tile), tile)
+            share_send[step, :, span] = jnp.dot(
+                flat, wo_s[step, :, span], preferred_element_type=f32
+            )
+            return carry
+
+        lax.fori_loop(0, columns // tile, columns_of, 0)
+        share_send[step, :, columns:] = low_o
+        if step < tp - 1:
+            share_copy(step).start()
+
+    take(3)
+    total = share_send[tp - 1]
+    for step in range(tp - 1):
+        share_copy(step).wait_recv()
+        total += share_recv[step]
+    parts = three_parts(total[:, columns : columns + rank])
+    last_width = ou_hbm.shape[1]
+    for i in range(dp):
+        span = slice(i * last_width, (i + 1) * last_width)
+        out_ref[:, span] = total[:, span] + adapter_scale * wide_product(parts, ou_s[i], rows)
+
+    for which in range(len(factors)):
+        for i in range(1, dp):
+            gather(which, i).wait_send()
+    for step in range(tp - 1):
+        low_copy(step).wait_send()
+        share_copy(step).wait_send()
+
+
+def on_device(
+    residual_hidden,
+    attention_norm_gain,
+    query_matrix,
+    key_matrix,
+    value_matrix,
+    output_matrix,
+    query_adapter_down,
+    query_adapter_up,
+    output_adapter_down,
+    output_adapter_up,
+    cached_rotated_keys,
+    cached_value_rows,
+    cache_fill_lengths,
+):
+    dp, tp = lax.axis_size("dp"), lax.axis_size("tp")
+    rows, features = residual_hidden.shape
+    rank = query_adapter_down.shape[1]
+    width = query_matrix.shape[1]
+    heads = width // HEAD_SIZE
+    groups = key_matrix.shape[1] // HEAD_SIZE
+    columns = output_matrix.shape[1] // tp
+    half = HEAD_SIZE // 2
+    lengths = cache_fill_lengths.astype(jnp.float32)[:, None]
+    inverse = jnp.exp(
+        jnp.arange(half, dtype=jnp.float32) * (-2.0 * math.log(rope_theta) / HEAD_SIZE)
+    )
+    angles = lengths * inverse[None, :]
+    cosine, sine = jnp.cos(angles), jnp.sin(angles)
+    table = jnp.concatenate(
+        [cosine, cosine, -sine, sine, jnp.broadcast_to(lengths, (rows, HEAD_SIZE))], axis=1
+    )
+    pieces = rows
+    bf16, f32 = jnp.bfloat16, jnp.float32
+    operands = (
+        residual_hidden,
+        attention_norm_gain.reshape(1, features),
+        table,
+        query_matrix,
+        key_matrix,
+        value_matrix,
+        output_matrix,
+        query_adapter_down,
+        query_adapter_up,
+        output_adapter_down,
+        output_adapter_up,
+        cached_rotated_keys,
+        cached_value_rows,
+    )
+    return pl.pallas_call(
+        functools.partial(kernel, dp, tp),
+        out_shape=jax.ShapeDtypeStruct((rows, columns), f32),
+        in_specs=[pl.BlockSpec(memory_space=pl.ANY)] * len(operands),
+        out_specs=pl.BlockSpec(memory_space=pltpu.VMEM),
+        scratch_shapes=[
+            pltpu.VMEM(residual_hidden.shape, bf16),
+            pltpu.VMEM((1, features), f32),
+            pltpu.VMEM(table.shape, f32),
+            pltpu.VMEM(query_matrix.shape, bf16),
+            pltpu.VMEM(key_matrix.shape, bf16),
+            pltpu.VMEM(value_matrix.shape, bf16),
+            pltpu.VMEM((tp, width, columns), bf16),
+            pltpu.VMEM((dp,) + query_adapter_down.shape, bf16),
+            pltpu.VMEM((dp,) + query_adapter_up.shape, bf16),
+            pltpu.VMEM((dp,) + output_adapter_down.shape, bf16),
+            pltpu.VMEM((dp,) + output_adapter_up.shape, bf16),
+            pltpu.VMEM(cached_rotated_keys.shape, bf16),
+            pltpu.VMEM(cached_value_rows.shape, bf16),
+            pltpu.VMEM((rows, features), bf16),
+            pltpu.VMEM((rows, heads, HEAD_SIZE), f32),
+            pltpu.VMEM((rows, groups + 1, HEAD_SIZE), f32),
+            pltpu.VMEM((rows, groups, HEAD_SIZE), f32),
+            pltpu.VMEM((heads, rows, HEAD_SIZE), f32),
+            pltpu.VMEM((rows, HEAD_SIZE), f32),
+            pltpu.VMEM((tp - 1, rows, HEAD_SIZE), f32),
+            pltpu.VMEM((tp, rows, columns + HEAD_SIZE), f32),
+            pltpu.VMEM((tp - 1, rows, columns + HEAD_SIZE), f32),
+            pltpu.SemaphoreType.DMA((3,)),
+            pltpu.SemaphoreType.DMA((3, pieces)),
+            pltpu.SemaphoreType.DMA((2, rows)),
+            pltpu.SemaphoreType.DMA((tp,)),
+            pltpu.SemaphoreType.DMA((4,)),
+            pltpu.SemaphoreType.DMA((4, dp)),
+            pltpu.SemaphoreType.DMA((4, dp)),
+            pltpu.SemaphoreType.DMA((tp - 1,)),
+            pltpu.SemaphoreType.DMA((tp - 1,)),
+            pltpu.SemaphoreType.DMA((tp - 1,)),
+            pltpu.SemaphoreType.DMA((tp - 1,)),
+        ],
+        compiler_params=pltpu.CompilerParams(
+            collective_id=0, has_side_effects=True, vmem_limit_bytes=56 * 1024 * 1024
+        ),
+    )(*operands)
+
+
 def solution(mesh):
     in_specs = (
         P("dp", None),
@@ -155,6 +603,11 @@
         P("dp"),
     )
     out_specs = P("dp", "tp")
+
+    def local(*arrays):
+        wide = arrays[7].shape[1] % HEAD_SIZE == 0 and arrays[9].shape[1] % HEAD_SIZE == 0
+        return (on_device if wide else on_device_narrow)(*arrays)
+
     return jax.shard_map(
-        on_device, mesh=mesh, in_specs=in_specs, out_specs=out_specs, check_vma=False
-    )
+        local, mesh=mesh, in_specs=in_specs, out_specs=out_specs, check_vma=False
+    )

time: 93.4 us -> 40.4 us (0.43)
  blocking collectives: 58.8 us -> 0 us
  Pallas kernels: 0 us -> 34.3 us
  matrix products: 16.2 us -> 0 us
  between operations: 13.5 us -> 0.02 us
  local copies, waits for them, and re-layouts: 0.3 us -> 5.03 us
  other arithmetic: 4.09 us -> 0.78 us
    all_gather x4 -> x0, blocking collectives: 38.5 us -> none  [the longest x1 10.7 us: on_device(): q_down_share = lax.all_gather(query_adapter_down, 'dp', axis=0, tiled=True)]
    pallas_call x0 -> x1, Pallas kernels: none -> 34.3 us  [on_device(): pl.pallas_call(functools.partial(kernel, dp, tp), out_shape=jax.ShapeDtyp...]
    psum x2 -> x0, blocking collectives: 20.3 us -> none  [the longest x1 11.9 us: on_device(): query_low_rank = lax.psum(partial_low, 'tp')]
    dot_general x11 -> x0, matrix products: 16.2 us -> none  [the longest x1 8.19 us: on_device(): jnp.dot(normalized_hidden, query_matrix, preferred_element_type=jnp.float32)]
    unnamed x22 -> x3, local copies, waits for them, and re-layouts: 0.28 us -> 4.29 us
    reduce_sum x2 -> x0, other arithmetic: 1.22 us -> none  [the longest x1 0.99 us: on_device(): jnp.mean(hidden_f * hidden_f, axis=-1, keepdims=True) + 1e-05]
    convert_element_type x3 -> x1, other arithmetic: 1.75 us -> 0.66 us  [on_device(): lengths = cache_fill_lengths.astype(jnp.float32)[:, None]]
  transfers between devices with their start and end apart: 1 -> 0, of which waited for: 0 -> 0; matrix products, arithmetic and copies ran while one was open for 0% -> 0% of each run, Pallas kernels for 0% -> 0%
where the time goes in v1:
time: 40.4 us; the launch traced here: 40.1 us
  Pallas kernels  34.3 us (85%)
  local copies, waits for them, and re-layouts  5.03 us (12%)
  other arithmetic  0.78 us (2%)
    pallas_call x1, Pallas kernels, on_device(): pl.pallas_call(functools.partial(kernel, dp, tp), out_shape=jax.ShapeDtyp...  34.3 us
    unnamed x3, local copies, waits for them, and re-layouts  4.29 us

profile of v1, /device:TPU:0, one launch (start us, length us, event | category | flops | bytes accessed | tf_op | source)
XLA Modules:
  0.0 40.1 jit_solution(9106871790755796101)
XLA Ops:
  0.0 0.7 %convert_element_type.3 = f32[8]{0:T(128)S(1)} convert(s32[8]{0:T(128)} %param.25) | non-fusion elementwise | flops 8 | bytes 64 | tf_op jit(solution)/shard_map/convert_element_type | solution.py:517
  0.7 0.1 broadcast_in_dim.2
  0.7 0.1 multiply_sine_fusion
  0.9 0.7 %concatenate.3.table_hbm = f32[8,384]{1,0:T(8,128)} concatenate(f32[8,64]{1,0:T(8,128)S(1)} %get-tuple-element.7, f32[8,64]{1,0:T(8,128)S(1)} %get-tuple-element.7, f32[8,64]{1,0:T(8,128)S(1)} %get-tuple-element.6, f32[8,64]{1,0:T(8,128)S(1)} %get-tuple-element.5, f32[8,128]{1,0:T(8,128)S(1)} %broadcast_in_dim.2), dimensions={1} | concatenate | bytes 24576 | tf_op jit(solution)/shard_map/concatenate | solution.py:523
  1.5 1.4 %copy.14.qd_hbm = bf16[128,64]{1,0:T(8,128)(2,1)} copy(bf16[128,64]{0,1:T(8,128)(2,1)} %param.19) | data formatting | bytes 32768 | tf_op args[6]
  3.0 1.5 %copy.15.od_hbm = bf16[256,64]{1,0:T(8,128)(2,1)} copy(bf16[256,64]{0,1:T(8,128)(2,1)} %param.21) | data formatting | bytes 65536 | tf_op args[8]
  4.4 34.3 %shard_map.127 = f32[8,1024]{1,0:T(8,128)} custom-call(bf16[8,4096]{1,0:T(8,128)(2,1)} %x_hbm.1, f32[1,4096]{1,0:T(1,128)} %bitcast.1, f32[8,384]{1,0:T(8,128)} %concatenate.3.table_hbm, bf16[4096,2048]{1,0:T(8,128)(2,1)} %wq_hbm.1, bf16[4096,256]{1,0:T(8,128)(2,1)} %wk_hbm.1, bf16[4096,256]{1,0:T(8,128)(2,1)} %wv_hbm.1, bf16[2048,4096]{1,0:T(8,128)(2,1)} %wo_hbm.1, ...), custom_call_target="tpu_custom_call" | custom-call | tf_op jit(solution)/shard_map/pallas_call | solution.py:543
  38.8 1.4 %copy.17 = f32[8,1024]{1,0:T(8,128)} copy(f32[8,1024]{1,0:T(8,128)} %shard_map.127) | data formatting | bytes 65536
  (1 shorter events, 0.0 us)

commit v2 on v1

--- a/solution.py
+++ b/solution.py
@@ -161,7 +161,7 @@
     tp,
     x_hbm,
     gain_hbm,
-    table_hbm,
+    lengths_hbm,
     wq_hbm,
     wk_hbm,
     wv_hbm,
@@ -172,9 +172,11 @@
     ou_hbm,
     k_hbm,
     v_hbm,
-    out_ref,
+    base_ref,
+    extra_ref,
     x_s,
     gain_s,
+    lengths_s,
     table_s,
     wq_s,
     wk_s,
@@ -202,6 +204,8 @@
     own_sem,
     gather_send,
     gather_recv,
+    relay_send,
+    relay_recv,
     low_send_sem,
     low_recv_sem,
     share_send_sem,
@@ -210,7 +214,7 @@
     d = lax.axis_index("dp")
     t = lax.axis_index("tp")
     rows, features = x_hbm.shape
-    rank = qd_hbm.shape[1]
+    rank = qd_hbm.shape[0]
     groups = k_hbm.shape[1]
     cache = k_hbm.shape[2]
     width = wq_hbm.shape[1]
@@ -218,12 +222,12 @@
     per_group = heads // groups
     pieces = w_sem.shape[1]
     depth = features // pieces
-    columns = out_ref.shape[1]
+    columns = base_ref.shape[1]
     f32, bf16 = jnp.float32, jnp.bfloat16
 
     small = [
         pltpu.make_async_copy(src, dst, in_sem.at[i])
-        for i, (src, dst) in enumerate(((x_hbm, x_s), (gain_hbm, gain_s), (table_hbm, table_s)))
+        for i, (src, dst) in enumerate(((x_hbm, x_s), (gain_hbm, gain_s), (lengths_hbm, lengths_s)))
     ]
     for copy in small:
         copy.start()
@@ -241,15 +245,20 @@
             for i, (src, dst) in enumerate(((k_hbm, k_s), (v_hbm, v_s)))
         ]
 
-    def out_copy(step):
+    halves = wo_sem.shape[1]
+    half_rows = width // halves
+
+    def out_copy(step, half):
         to = lax.rem(t + 1 + step, tp)
+        span = pl.ds(pl.multiple_of(half * half_rows, half_rows), half_rows)
         return pltpu.make_async_copy(
-            wo_hbm.at[:, pl.ds(pl.multiple_of(to * columns, columns), columns)],
-            wo_s.at[step],
-            wo_sem.at[step],
-        )
-
-    for k in range(pieces):
+            wo_hbm.at[span, pl.ds(pl.multiple_of(to * columns, columns), columns)],
+            wo_s.at[step, span],
+            wo_sem.at[step, half],
+        )
+
+    ahead = pieces // 2
+    for k in range(ahead):
         for copy in weight_copies(k):
             copy.start()
 
@@ -260,20 +269,18 @@
     for copy in own:
         copy.start()
 
+    chips = dp // 2
+    sibling = d + 1 - 2 * lax.rem(d, 2)
+
+    def same_core(i):
+        return lax.rem(d + 2 * i, dp)
+
     barrier = pltpu.get_barrier_semaphore()
-    for i in range(1, dp):
+    peers = [(same_core(i), t) for i in range(1, chips)] + [(sibling, t)]
+    peers += [(d, lax.rem(t + i, tp)) for i in range(1, tp)]
+    for peer in peers:
         pl.semaphore_signal(
-            barrier,
-            inc=1,
-            device_id=(lax.rem(d + i, dp), t),
-            device_id_type=pl.DeviceIdType.MESH,
-        )
-    for i in range(1, tp):
-        pl.semaphore_signal(
-            barrier,
-            inc=1,
-            device_id=(d, lax.rem(t + i, tp)),
-            device_id_type=pl.DeviceIdType.MESH,
+            barrier, inc=1, device_id=peer, device_id_type=pl.DeviceIdType.MESH
         )
 
     for copy in small:
@@ -285,7 +292,25 @@
         * gain_s[...]
     ).astype(bf16)
 
-    pl.semaphore_wait(barrier, dp - 1 + tp - 1)
+    lengths = jnp.sum(
+        jnp.where(
+            lax.broadcasted_iota(jnp.int32, (rows, rows), 0)
+            == lax.broadcasted_iota(jnp.int32, (rows, rows), 1),
+            jnp.broadcast_to(lengths_s[...].astype(f32), (rows, rows)),
+            0.0,
+        ),
+        axis=1,
+        keepdims=True,
+    )
+    lane = lax.broadcasted_iota(jnp.int32, (rows, HEAD_SIZE), 1)
+    first = lane < HEAD_SIZE // 2
+    number = jnp.where(first, lane, lane - HEAD_SIZE // 2).astype(f32)
+    angles = lengths * jnp.exp(number * (-2.0 * math.log(rope_theta) / HEAD_SIZE))
+    table_s[:, :HEAD_SIZE] = jnp.cos(angles)
+    table_s[:, HEAD_SIZE:] = jnp.where(first, -jnp.sin(angles), jnp.sin(angles))
+    key_s[:, groups, :] = jnp.broadcast_to(lengths, (rows, HEAD_SIZE))
+
+    pl.semaphore_wait(barrier, len(peers))
 
     def gather(which, i):
         src, dst = factors[which]
@@ -294,7 +319,19 @@
             dst_ref=dst.at[d],
             send_sem=gather_send.at[which, i],
             recv_sem=gather_recv.at[which, i],
-            device_id=(lax.rem(d + i, dp), t),
+            device_id=(same_core(i), t),
+            device_id_type=pl.DeviceIdType.MESH,
+        )
+
+    def relayed(which, i, core):
+        dst = factors[which][1]
+        slot = lax.rem(core + dp - 2 * i, dp)
+        return pltpu.make_async_remote_copy(
+            src_ref=dst.at[slot] if i else factors[which][0],
+            dst_ref=dst.at[slot],
+            send_sem=relay_send.at[which, i],
+            recv_sem=relay_recv.at[which, i],
+            device_id=(sibling, t),
             device_id_type=pl.DeviceIdType.MESH,
         )
 
@@ -302,27 +339,46 @@
         src, dst = factors[which]
         return pltpu.make_async_remote_copy(
             src_ref=src,
-            dst_ref=dst.at[lax.rem(d + dp - i, dp)],
+            dst_ref=dst.at[lax.rem(d + dp - 2 * i, dp)],
             send_sem=gather_send.at[which, i],
             recv_sem=gather_recv.at[which, i],
-            device_id=(lax.rem(d + i, dp), t),
+            device_id=(same_core(i), t),
             device_id_type=pl.DeviceIdType.MESH,
         )
 
-    for which in range(len(factors)):
-        for i in range(1, dp):
+    def spread(which):
+        for i in range(1, chips):
             gather(which, i).start()
+        relayed(which, 0, d).start()
+
+    def relay(which):
+        for i in range(1, chips):
+            arrived(which, i).wait_recv()
+            relayed(which, i, d).start()
 
     def take(which):
         own[which].wait()
-        for i in range(1, dp):
-            arrived(which, i).wait_recv()
+        for i in range(chips):
+            relayed(which, i, sibling).wait_recv()
+
+    spread(0)
+    spread(1)
 
     def project(k, totals):
         for copy in weight_copies(k):
             copy.wait()
-        for copy in cache_copies(k):
-            copy.start()
+
+        @pl.when(k < pieces - ahead)
+        def _():
+            for copy in weight_copies(k + ahead):
+                copy.start()
+
+        @pl.when(k >= pieces - ahead)
+        def _():
+            for u in range(2):
+                for copy in cache_copies((k - (pieces - ahead)) * 2 + u):
+                    copy.start()
+
         span = pl.ds(pl.multiple_of(k * depth, depth), depth)
         block = normed_s[:, span]
         return tuple(
@@ -333,13 +389,18 @@
     totals = tuple(jnp.zeros((rows, w.shape[1]), f32) for w in (wq_s, wk_s, wv_s))
     totals = lax.fori_loop(0, pieces // 2, project, totals)
 
+    relay(0)
+    relay(1)
     take(0)
-    part_width = qd_hbm.shape[0]
+    part_width = qd_hbm.shape[1]
     part = jnp.zeros((rows, rank), f32)
     for i in range(dp):
         at = pl.multiple_of((i * tp + t) * part_width, part_width)
-        part += jnp.dot(
-            normed_s[:, pl.ds(at, part_width)], qd_s[i], preferred_element_type=f32
+        part += lax.dot_general(
+            normed_s[:, pl.ds(at, part_width)],
+            qd_s[i],
+            (((1,), (1,)), ((), ())),
+            preferred_element_type=f32,
         )
     low_send[...] = jnp.concatenate(
         [part, jnp.zeros((rows, HEAD_SIZE - rank), f32)], axis=1
@@ -360,11 +421,8 @@
 
     totals = lax.fori_loop(pieces // 2, pieces, project, totals)
     query_total, key_total, value_total = totals
-    for step in range(tp):
-        out_copy(step).start()
-
     cosine = table_s[:, :HEAD_SIZE]
-    sine = table_s[:, HEAD_SIZE : 2 * HEAD_SIZE]
+    sine = table_s[:, HEAD_SIZE:]
 
     def turned(vectors):
         rolled = pltpu.roll(vectors, HEAD_SIZE // 2, 1)
@@ -375,8 +433,8 @@
         key_s[:, g, :] = turned(key_total[:, span])
         value_s[:, g, :] = value_total[:, span].astype(bf16).astype(f32)
 
-    key_s[:, groups, :] = table_s[:, 2 * HEAD_SIZE :]
-
+    spread(2)
+    spread(3)
     take(1)
     low = low_send[...]
     for step in range(tp - 1):
@@ -395,11 +453,15 @@
 
     scale = HEAD_SIZE ** (-0.5)
     at_once = 2
+    units_each = tp * halves * at_once // rows
 
     def attend(step, carry):
         for u in range(at_once):
             for copy in cache_copies(step * at_once + u):
                 copy.wait()
+        for u in range(units_each):
+            unit = step * units_each + u
+            out_copy(unit // halves, unit % halves).start()
         place = lax.broadcasted_iota(jnp.int32, (per_group, cache), 1).astype(f32)
         results = []
         for u in range(at_once):
@@ -433,16 +495,22 @@
             attn_s[g * per_group : (g + 1) * per_group, r, :] = mixed
         return carry
 
-    lax.fori_loop(0, rows // at_once, attend, 0)
+    lax.fori_loop(0, rows // at_once // 2, attend, 0)
+    relay(2)
+    relay(3)
+    lax.fori_loop(rows // at_once // 2, rows // at_once, attend, 0)
 
     flat = jnp.concatenate([attn_s[h] for h in range(heads)], axis=1).astype(bf16)
 
     take(2)
-    down_rows = od_hbm.shape[0]
+    down_rows = od_hbm.shape[1]
     low_o = jnp.zeros((rows, rank), f32)
     for i in range(dp):
-        low_o += jnp.dot(
-            flat[:, i * down_rows : (i + 1) * down_rows], od_s[i], preferred_element_type=f32
+        low_o += lax.dot_general(
+            flat[:, i * down_rows : (i + 1) * down_rows],
+            od_s[i],
+            (((1,), (1,)), ((), ())),
+            preferred_element_type=f32,
         )
     low_o = jnp.concatenate([low_o, jnp.zeros((rows, HEAD_SIZE - rank), f32)], axis=1)
 
@@ -458,7 +526,8 @@
 
     tile = 256
     for step in range(tp):
-        out_copy(step).wait()
+        for half in range(halves):
+            out_copy(step, half).wait()
 
         def columns_of(c, carry, step=step):
             span = pl.ds(pl.multiple_of(c * tile, tile), tile)
@@ -481,11 +550,14 @@
     last_width = ou_hbm.shape[1]
     for i in range(dp):
         span = slice(i * last_width, (i + 1) * last_width)
-        out_ref[:, span] = total[:, span] + adapter_scale * wide_product(parts, ou_s[i], rows)
+        extra_ref[:, span] = adapter_scale * wide_product(parts, ou_s[i], rows)
+    base_ref[...] = total[:, :columns]
 
     for which in range(len(factors)):
-        for i in range(1, dp):
+        for i in range(1, chips):
             gather(which, i).wait_send()
+        for i in range(chips):
+            relayed(which, i, d).wait_send()
     for step in range(tp - 1):
         low_copy(step).wait_send()
         share_copy(step).wait_send()
@@ -508,54 +580,44 @@
 ):
     dp, tp = lax.axis_size("dp"), lax.axis_size("tp")
     rows, features = residual_hidden.shape
-    rank = query_adapter_down.shape[1]
     width = query_matrix.shape[1]
     heads = width // HEAD_SIZE
     groups = key_matrix.shape[1] // HEAD_SIZE
     columns = output_matrix.shape[1] // tp
-    half = HEAD_SIZE // 2
-    lengths = cache_fill_lengths.astype(jnp.float32)[:, None]
-    inverse = jnp.exp(
-        jnp.arange(half, dtype=jnp.float32) * (-2.0 * math.log(rope_theta) / HEAD_SIZE)
-    )
-    angles = lengths * inverse[None, :]
-    cosine, sine = jnp.cos(angles), jnp.sin(angles)
-    table = jnp.concatenate(
-        [cosine, cosine, -sine, sine, jnp.broadcast_to(lengths, (rows, HEAD_SIZE))], axis=1
-    )
     pieces = rows
     bf16, f32 = jnp.bfloat16, jnp.float32
     operands = (
         residual_hidden,
         attention_norm_gain.reshape(1, features),
-        table,
+        cache_fill_lengths.reshape(1, rows),
         query_matrix,
         key_matrix,
         value_matrix,
         output_matrix,
-        query_adapter_down,
+        query_adapter_down.T,
         query_adapter_up,
-        output_adapter_down,
+        output_adapter_down.T,
         output_adapter_up,
         cached_rotated_keys,
         cached_value_rows,
     )
-    return pl.pallas_call(
+    base, extra = pl.pallas_call(
         functools.partial(kernel, dp, tp),
-        out_shape=jax.ShapeDtypeStruct((rows, columns), f32),
+        out_shape=[jax.ShapeDtypeStruct((rows, columns), f32)] * 2,
         in_specs=[pl.BlockSpec(memory_space=pl.ANY)] * len(operands),
-        out_specs=pl.BlockSpec(memory_space=pltpu.VMEM),
+        out_specs=[pl.BlockSpec(memory_space=pltpu.VMEM)] * 2,
         scratch_shapes=[
             pltpu.VMEM(residual_hidden.shape, bf16),
             pltpu.VMEM((1, features), f32),
-            pltpu.VMEM(table.shape, f32),
+            pltpu.VMEM((1, rows), jnp.int32),
+            pltpu.VMEM((rows, 2 * HEAD_SIZE), f32),
             pltpu.VMEM(query_matrix.shape, bf16),
             pltpu.VMEM(key_matrix.shape, bf16),
             pltpu.VMEM(value_matrix.shape, bf16),
             pltpu.VMEM((tp, width, columns), bf16),
-            pltpu.VMEM((dp,) + query_adapter_down.shape, bf16),
+            pltpu.VMEM((dp,) + query_adapter_down.shape[::-1], bf16),
             pltpu.VMEM((dp,) + query_adapter_up.shape, bf16),
-            pltpu.VMEM((dp,) + output_adapter_down.shape, bf16),
+            pltpu.VMEM((dp,) + output_adapter_down.shape[::-1], bf16),
             pltpu.VMEM((dp,) + output_adapter_up.shape, bf16),
             pltpu.VMEM(cached_rotated_keys.shape, bf16),
             pltpu.VMEM(cached_value_rows.shape, bf16),
@@ -571,10 +633,12 @@
             pltpu.SemaphoreType.DMA((3,)),
             pltpu.SemaphoreType.DMA((3, pieces)),
             pltpu.SemaphoreType.DMA((2, rows)),
-            pltpu.SemaphoreType.DMA((tp,)),
+            pltpu.SemaphoreType.DMA((tp, 2)),
             pltpu.SemaphoreType.DMA((4,)),
-            pltpu.SemaphoreType.DMA((4, dp)),
-            pltpu.SemaphoreType.DMA((4, dp)),
+            pltpu.SemaphoreType.DMA((4, dp // 2)),
+            pltpu.SemaphoreType.DMA((4, dp // 2)),
+            pltpu.SemaphoreType.DMA((4, dp // 2)),
+            pltpu.SemaphoreType.DMA((4, dp // 2)),
             pltpu.SemaphoreType.DMA((tp - 1,)),
             pltpu.SemaphoreType.DMA((tp - 1,)),
             pltpu.SemaphoreType.DMA((tp - 1,)),
@@ -584,6 +648,7 @@
             collective_id=0, has_side_effects=True, vmem_limit_bytes=56 * 1024 * 1024
         ),
     )(*operands)
+    return base + extra
 
 
 def solution(mesh):

time: 40.4 us -> 32.5 us (0.80)
  local copies, waits for them, and re-layouts: 5.03 us -> 0 us
  Pallas kernels: 34.3 us -> 30.9 us
  other arithmetic: 0.78 us -> 1.4 us
    unnamed x3 -> x0, local copies, waits for them, and re-layouts: 4.29 us -> none
    pallas_call x1, Pallas kernels: 34.3 us -> 30.9 us  [on_device(): pl.pallas_call(functools.partial(kernel, dp, tp), out_shape=[jax.ShapeDty...]
    add x0 -> x1, other arithmetic: none -> 1.4 us  [on_device(): return base + extra]
    concatenate x1 -> x0, local copies, waits for them, and re-layouts: 0.68 us -> none  [on_device(): jnp.concatenate([cosine, cosine, -sine, sine, jnp.broadcast_to(lengths, (...]
    convert_element_type x1 -> x0, other arithmetic: 0.66 us -> none  [on_device(): lengths = cache_fill_lengths.astype(jnp.float32)[:, None]]
where the time goes in v2:
time: 32.5 us; the launch traced here: 32.3 us
  Pallas kernels  30.9 us (95%)
  other arithmetic  1.4 us (4%)
    pallas_call x1, Pallas kernels, on_device(): pl.pallas_call(functools.partial(kernel, dp, tp), out_shape=[jax.ShapeDty...  30.9 us
    add x1, other arithmetic, on_device(): return base + extra  1.4 us

profile of v2, /device:TPU:0, one launch (start us, length us, event | category | flops | bytes accessed | tf_op | source)
XLA Modules:
  0.0 32.3 jit_solution(1794179789333223855)
XLA Ops:
  0.0 30.9 %shard_map.127 = (f32[8,1024]{1,0:T(8,128)}, f32[8,1024]{1,0:T(8,128)}) custom-call(bf16[8,4096]{1,0:T(8,128)(2,1)} %x_hbm.1, f32[1,4096]{1,0:T(1,128)} %bitcast.5, s32[1,8]{1,0:T(1,128)} %bitcast.7, bf16[4096,2048]{1,0:T(8,128)(2,1)} %wq_hbm.1, bf16[4096,256]{1,0:T(8,128)(2,1)} %wk_hbm.1, bf16[4096,256]{1,0:T(8,128)(2,1)} %wv_hbm.1, ...), custom_call_target="tpu_custom_call" | custom-call | tf_op jit(solution)/shard_map/pallas_call | solution.py:604
  30.9 1.4 %add.3 = f32[8,1024]{1,0:T(8,128)} add(f32[8,1024]{1,0:T(8,128)} %get-tuple-element.7, f32[8,1024]{1,0:T(8,128)} %get-tuple-element.8) | non-fusion elementwise | flops 8192 | bytes 98304 | tf_op jit(solution)/shard_map/add | solution.py:651

commit v3 on v2

--- a/solution.py
+++ b/solution.py
@@ -452,7 +452,7 @@
             )
 
     scale = HEAD_SIZE ** (-0.5)
-    at_once = 2
+    at_once = 4
     units_each = tp * halves * at_once // rows
 
     def attend(step, carry):
@@ -462,37 +462,63 @@
         for u in range(units_each):
             unit = step * units_each + u
             out_copy(unit // halves, unit % halves).start()
-        place = lax.broadcasted_iota(jnp.int32, (per_group, cache), 1).astype(f32)
-        results = []
-        for u in range(at_once):
-            r = step * at_once + u
-            length = key_s[r, groups : groups + 1, :][:, :1]
-            for g in range(groups):
-                query = q_s[r, g * per_group : (g + 1) * per_group, :]
-                scores = (
-                    lax.dot_general(
-                        query.astype(bf16),
-                        k_s[r, g],
-                        (((1,), (1,)), ((), ())),
-                        preferred_element_type=f32,
+        pairs = [(step * at_once + u, g) for u in range(at_once) for g in range(groups)]
+        count = len(pairs) * per_group
+
+        def stacked(blocks):
+            return jnp.concatenate(blocks, axis=0)
+
+        def spread_out(ref, place):
+            return stacked(
+                [
+                    jnp.broadcast_to(
+                        ref[r, pl.ds(g if place is None else place, 1), :],
+                        (per_group, HEAD_SIZE),
                     )
-                    * scale
+                    for r, g in pairs
+                ]
+            )
+
+        queries = [q_s[r, g * per_group : (g + 1) * per_group, :] for r, g in pairs]
+        scores = stacked(
+            [
+                lax.dot_general(
+                    query.astype(bf16),
+                    k_s[r, g],
+                    (((1,), (1,)), ((), ())),
+                    preferred_element_type=f32,
                 )
-                scores = jnp.where(place < length, scores, -jnp.inf)
-                mine = (
-                    jnp.sum(query * key_s[r, g : g + 1, :], axis=-1, keepdims=True) * scale
+                for query, (r, g) in zip(queries, pairs)
+            ]
+        )
+        mine = (
+            jnp.sum(stacked(queries) * spread_out(key_s, None), axis=-1, keepdims=True) * scale
+        )
+        reach = spread_out(key_s, groups)[:, :1]
+        seat = lax.broadcasted_iota(jnp.int32, (count, cache), 1).astype(f32)
+        scores = jnp.where(seat < reach, scores * scale, -jnp.inf)
+        top = jnp.maximum(jnp.max(scores, axis=-1, keepdims=True), mine)
+        powers = jnp.exp(scores - top)
+        my_power = jnp.exp(mine - top)
+        inverse = 1.0 / (jnp.sum(powers, axis=-1, keepdims=True) + my_power)
+        weights = powers * inverse
+        my_weight = (my_power * inverse).astype(bf16).astype(f32)
+        mixed = stacked(
+            [
+                jnp.dot(
+                    weights[n * per_group : (n + 1) * per_group].astype(bf16),
+                    v_s[r, g],
+                    preferred_element_type=f32,
                 )
-                top = jnp.maximum(jnp.max(scores, axis=-1, keepdims=True), mine)
-                powers = jnp.exp(scores - top)
-                my_power = jnp.exp(mine - top)
-                inverse = 1.0 / (jnp.sum(powers, axis=-1, keepdims=True) + my_power)
-                weights = (powers * inverse).astype(bf16)
-                my_weight = (my_power * inverse).astype(bf16).astype(f32)
-                mixed = jnp.dot(weights, v_s[r, g], preferred_element_type=f32)
-                mixed = mixed + my_weight * value_s[r, g : g + 1, :]
-                results.append((r, g, mixed.astype(bf16).astype(f32)))
-        for r, g, mixed in results:
-            attn_s[g * per_group : (g + 1) * per_group, r, :] = mixed
+                for n, (r, g) in enumerate(pairs)
+            ]
+        )
+        mixed = mixed + my_weight * spread_out(value_s, None)
+        mixed = mixed.astype(bf16).astype(f32)
+        for n, (r, g) in enumerate(pairs):
+            attn_s[g * per_group : (g + 1) * per_group, r, :] = mixed[
+                n * per_group : (n + 1) * per_group
+            ]
         return carry
 
     lax.fori_loop(0, rows // at_once // 2, attend, 0)
@@ -603,7 +629,7 @@
     )
     base, extra = pl.pallas_call(
         functools.partial(kernel, dp, tp),
-        out_shape=[jax.ShapeDtypeStruct((rows, columns), f32)] * 2,
+        out_shape=[pltpu.VMEM((rows, columns), f32)] * 2,
         in_specs=[pl.BlockSpec(memory_space=pl.ANY)] * len(operands),
         out_specs=[pl.BlockSpec(memory_space=pltpu.VMEM)] * 2,
         scratch_shapes=[

time: 32.5 us -> 28.7 us (0.88)
  Pallas kernels: 30.9 us -> 27.9 us
  other arithmetic: 1.4 us -> 0.62 us
    pallas_call x1, Pallas kernels: 30.9 us -> 27.9 us  [on_device(): pl.pallas_call(functools.partial(kernel, dp, tp), out_shape=[pltpu.VMEM((...]
    add x1, other arithmetic: 1.4 us -> 0.62 us  [on_device(): return base + extra]
where the time goes in v3:
time: 28.7 us; the launch traced here: 28.5 us
  Pallas kernels  27.9 us (97%)
  other arithmetic  0.62 us (2%)
    pallas_call x1, Pallas kernels, on_device(): pl.pallas_call(functools.partial(kernel, dp, tp), out_shape=[pltpu.VMEM((...  27.9 us
    add x1, other arithmetic, on_device(): return base + extra  0.62 us

profile of v3, /device:TPU:0, one launch (start us, length us, event | category | flops | bytes accessed | tf_op | source)
XLA Modules:
  0.0 28.5 jit_solution(6203898871039648218)
XLA Ops:
  0.0 27.9 %shard_map.127 = (f32[8,1024]{1,0:T(8,128)S(1)}, f32[8,1024]{1,0:T(8,128)S(1)}) custom-call(bf16[8,4096]{1,0:T(8,128)(2,1)} %x_hbm.1, f32[1,4096]{1,0:T(1,128)} %bitcast.5, s32[1,8]{1,0:T(1,128)} %bitcast.7, bf16[4096,2048]{1,0:T(8,128)(2,1)} %wq_hbm.1, bf16[4096,256]{1,0:T(8,128)(2,1)} %wk_hbm.1, bf16[4096,256]{1,0:T(8,128)(2,1)} %wv_hbm.1, ...), custom_call_target="tpu_custom_call" | custom-call | tf_op jit(solution)/shard_map/pallas_call | solution.py:630
  27.9 0.6 %add.3 = f32[8,1024]{1,0:T(8,128)} add(f32[8,1024]{1,0:T(8,128)S(1)} %get-tuple-element.7, f32[8,1024]{1,0:T(8,128)S(1)} %get-tuple-element.8) | non-fusion elementwise | flops 8192 | bytes 98304 | tf_op jit(solution)/shard_map/add | solution.py:677

commit v4 on v3

--- a/solution.py
+++ b/solution.py
@@ -390,7 +390,6 @@
     totals = lax.fori_loop(0, pieces // 2, project, totals)
 
     relay(0)
-    relay(1)
     take(0)
     part_width = qd_hbm.shape[1]
     part = jnp.zeros((rows, rank), f32)
@@ -418,6 +417,9 @@
 
     for step in range(tp - 1):
         low_copy(step).start()
+    relay(1)
+    spread(2)
+    spread(3)
 
     totals = lax.fori_loop(pieces // 2, pieces, project, totals)
     query_total, key_total, value_total = totals
@@ -433,9 +435,9 @@
         key_s[:, g, :] = turned(key_total[:, span])
         value_s[:, g, :] = value_total[:, span].astype(bf16).astype(f32)
 
-    spread(2)
-    spread(3)
     take(1)
+    for unit in range(tp * halves):
+        out_copy(unit // halves, unit % halves).start()
     low = low_send[...]
     for step in range(tp - 1):
         low_copy(step).wait_recv()
@@ -453,15 +455,11 @@
 
     scale = HEAD_SIZE ** (-0.5)
     at_once = 4
-    units_each = tp * halves * at_once // rows
 
     def attend(step, carry):
         for u in range(at_once):
             for copy in cache_copies(step * at_once + u):
                 copy.wait()
-        for u in range(units_each):
-            unit = step * units_each + u
-            out_copy(unit // halves, unit % halves).start()
         pairs = [(step * at_once + u, g) for u in range(at_once) for g in range(groups)]
         count = len(pairs) * per_group
 
@@ -550,7 +548,7 @@
             device_id_type=pl.DeviceIdType.MESH,
         )
 
-    tile = 256
+    tile = 512
     for step in range(tp):
         for half in range(halves):
             out_copy(step, half).wait()

time: 28.7 us -> 26.3 us (0.916)
  Pallas kernels: 27.9 us -> 25.5 us
    pallas_call x1, Pallas kernels: 27.9 us -> 25.5 us  [on_device(): pl.pallas_call(functools.partial(kernel, dp, tp), out_shape=[pltpu.VMEM((...]
where the time goes in v4:
time: 26.3 us; the launch traced here: 26.2 us
  Pallas kernels  25.5 us (97%)
  other arithmetic  0.62 us (2%)
    pallas_call x1, Pallas kernels, on_device(): pl.pallas_call(functools.partial(kernel, dp, tp), out_shape=[pltpu.VMEM((...  25.5 us
    add x1, other arithmetic, on_device(): return base + extra  0.62 us

profile of v4, /device:TPU:0, one launch (start us, length us, event | category | flops | bytes accessed | tf_op | source)
XLA Modules:
  0.0 26.2 jit_solution(12191473186313494068)
XLA Ops:
  0.0 25.5 %shard_map.127 = (f32[8,1024]{1,0:T(8,128)S(1)}, f32[8,1024]{1,0:T(8,128)S(1)}) custom-call(bf16[8,4096]{1,0:T(8,128)(2,1)} %x_hbm.1, f32[1,4096]{1,0:T(1,128)} %bitcast.5, s32[1,8]{1,0:T(1,128)} %bitcast.7, bf16[4096,2048]{1,0:T(8,128)(2,1)} %wq_hbm.1, bf16[4096,256]{1,0:T(8,128)(2,1)} %wk_hbm.1, bf16[4096,256]{1,0:T(8,128)(2,1)} %wv_hbm.1, ...), custom_call_target="tpu_custom_call" | custom-call | tf_op jit(solution)/shard_map/pallas_call | solution.py:628
  25.6 0.6 %add.3 = f32[8,1024]{1,0:T(8,128)} add(f32[8,1024]{1,0:T(8,128)S(1)} %get-tuple-element.7, f32[8,1024]{1,0:T(8,128)S(1)} %get-tuple-element.8) | non-fusion elementwise | flops 8192 | bytes 98304 | tf_op jit(solution)/shard_map/add | solution.py:675
